TPU v7x, 128 devices: a whole 4x4x4 slice. The times are simulated.
128 devices in a mesh: row: 16 (over z_hi, y, core), col: 8 (over z_lo, x).
Axes of the slice: x: 4, y: 4, z: 4 (z_hi: 2, z_lo: 2; z = z_hi * 2 + z_lo), core: 2. Of those that a mesh axis runs over, the one named last changes fastest.
Arguments:
- blocks: bfloat16 [512, 1024, 128], P('row', 'col'), may hold values from -6 to 6
- block_atom: int32 [512, 8], P('row', 'col'), may hold values from 0 to 63, as said below
- block_col: int32 [512, 8], P('row', 'col'), may hold values from 0 to 7
- block_count: int32 [16, 8], P('row', 'col'), may hold values from 0 to 32, as said below
Outputs:
- sign_step: float32 [8192, 8192], P('row', 'col')
Inputs may be any that keep to these rules, and one draw needn't show every extreme that they name: Entries from block_count on are padding. `block_atom`: used entries of one grid column name distinct blocks; one owner's list names at most 2 blocks of the block rows of any one grid row.
All inputs are finite; a program needn't handle non-finite values.
Results may differ from a plain program's by a relative error of at most 0.0045.
Values may be sent and summed in bfloat16 or wider, within the bound.
No kernel may reach another device: no remote copies, remote signals or barrier semaphores. Data moves between devices by JAX's collectives and lax.ppermute only.
A program may use at most 128 MiB of HBM per device.

v0:
```python
import jax
import jax.numpy as jnp
from jax import lax
from jax.sharding import PartitionSpec as P

BR = 4


def local(blocks, block_atom, block_col, block_count):
    slot_count, width, _ = blocks.shape
    row_devices = lax.axis_size("row")
    tile_cols = BR * row_devices // lax.axis_size("col")
    tile_size = BR * tile_cols
    flattened = blocks.reshape(slot_count, width * width)
    atom_ids = block_atom[:, 0]
    column_ids = block_col[:, 0]
    my_row = lax.axis_index("row")
    tile_index = jnp.arange(tile_size, dtype=jnp.int32)
    gathered, all_atoms, all_columns, all_counts = (
        lax.all_gather(flattened, "row", axis=0, tiled=True),
        lax.all_gather(atom_ids, "row", axis=0, tiled=True),
        lax.all_gather(column_ids, "row", axis=0, tiled=True),
        lax.all_gather(block_count[:, 0], "row", axis=0, tiled=True),
    )
    slot_position = jnp.arange(row_devices * slot_count, dtype=jnp.int32) % slot_count
    is_live = slot_position < jnp.repeat(all_counts, slot_count)
    is_mine = is_live & (all_atoms // BR == my_row)
    position = all_atoms % BR * tile_cols + all_columns
    select = (is_mine[None, :] & (position[None, :] == tile_index[:, None])).astype(jnp.bfloat16)
    tile_blocks = jnp.dot(select, gathered, preferred_element_type=jnp.float32).astype(jnp.bfloat16)
    matrix = (
        tile_blocks.reshape(BR, tile_cols, width, width)
        .transpose(0, 2, 1, 3)
        .reshape(BR * width, tile_cols * width)
    )
    row_strip = lax.all_gather(matrix, "col", axis=1, tiled=True)
    factor = 0.5 / row_strip.shape[1]

    def add_left(shard_piece):
        return jnp.dot(row_strip, shard_piece, preferred_element_type=jnp.float32)

    square = add_left(lax.all_gather(matrix, "row", axis=0, tiled=True))
    half_square = (square * factor).astype(jnp.bfloat16)
    product = add_left(lax.all_gather(half_square, "row", axis=0, tiled=True))
    return 1.5 * matrix.astype(jnp.float32) - product


def solution(mesh):
    placed = (P("row", "col", None), P("row", "col"), P("row", "col"), P("row", "col"))
    return jax.shard_map(
        local, mesh=mesh, in_specs=placed, out_specs=P("row", "col"), check_vma=False
    )
```

profile of v0, /device:TPU:0, one launch (start us, length us, event | category | flops | bytes accessed | tf_op | source)
XLA Modules:
  0.0 479.6 jit_solution(15783882242483573240)
XLA Ops:
  6.5 0.0 all-gather.8.cloned.1.call-start
  6.5 2.9 copy.12
  9.4 0.0 all-gather.8.cloned.1.call-update
  9.4 0.0 all-gather.10.cloned.1.call-start
  10.1 1.3 dynamic-slice
  12.1 0.6 bitcast_dynamic-update-slice_fusion.2
  12.7 0.8 bitcast_dynamic-update-slice_fusion
  13.5 0.7 bitcast_dynamic-update-slice_fusion.1
  14.2 15.3 %all-reduce.3 = (s32[512]{0:T(512)S(1)}, s32[512]{0:T(512)S(1)}, s32[16]{0:T(128)S(1)}) all-reduce(s32[512]{0:T(512)S(1)} %bitcast_dynamic-update-slice_fusion, s32[512]{0:T(512)S(1)} %bitcast_dynamic-update-slice_fusion.1, s32[16]{0:T(128)S(1)} %bitcast_dynamic-update-slice_fusion.2), channel_id=4, replica_groups=mesh['row'=16,'col'=8] {'row'}, use_global_device_ids=true, to_apply=%add.2 | all-reduce | flops 1040 | bytes 8320 | tf_op jit(solution)/shard_map/all_gather | solution.py:22
  29.5 0.1 broadcast_in_dim.2
  29.6 0.1 reshape.14
  29.7 92.9 %all-gather.8.cloned.1.call-done = bf16[512,16384]{1,0:T(8,128)(2,1)} async-done(((bf16[32,16384]{1,0:T(8,128)(2,1)}), bf16[512,16384]{1,0:T(8,128)(2,1)}) %all-gather.8.cloned.1.call-update) | async-done | bytes 16777232 | tf_op jit(solution)/shard_map/all_gather | solution.py:20
  122.6 8.6 %convolution_convert_fusion = bf16[32,16384]{1,0:T(8,128)(2,1)S(1)} fusion(bf16[512,16384]{1,0:T(8,128)(2,1)} %all-gather.8.cloned.1.call-done, s32[512]{0:T(512)S(1)} %fusion.7, pred[512]{0:T(512)(128)(4,1)S(1)} %fusion.12), kind=kOutput, calls=%fused_computation | convolution fusion | flops 537427968 | bytes 17828352 | tf_op jit(solution)/shard_map/dot_general | solution.py:30
  131.3 1.2 copy.11
  132.5 0.0 all-gather.10.cloned.1.call-update
  132.6 0.0 all-gather.12.cloned.1.call-start
  132.6 0.7 all-gather.12.cloned.1.call-update
  133.3 0.0 all-gather.14.cloned.1.call-start
  133.3 88.8 %all-gather.10.cloned.1.call-done = bf16[512,8192]{1,0:T(8,128)(2,1)} async-done(((bf16[512,1024]{1,0:T(8,128)(2,1)}), bf16[512,8192]{1,0:T(8,128)(2,1)}) %all-gather.10.cloned.1.call-update) | async-done | bytes 8388624 | tf_op jit(solution)/shard_map/all_gather | solution.py:36
  222.2 111.6 %all-gather.12.cloned.1.call-done = bf16[8192,1024]{1,0:T(8,128)(2,1)} async-done(((bf16[512,1024]{1,0:T(8,128)(2,1)}), bf16[8192,1024]{1,0:T(8,128)(2,1)}) %all-gather.12.cloned.1.call-update) | async-done | bytes 16777232 | tf_op jit(solution)/shard_map/all_gather | solution.py:42
  333.8 15.6 %multiply_convert_fusion = bf16[512,1024]{1,0:T(8,128)(2,1)} fusion(bf16[512,8192]{1,0:T(8,128)(2,1)} %all-gather.10.cloned.1.call-done, bf16[8192,1024]{1,0:T(8,128)(2,1)} %all-gather.12.cloned.1.call-done), kind=kOutput, calls=%fused_computation.1 | convolution fusion | flops 8590983168 | bytes 26214400 | tf_op jit(solution)/shard_map/dot_general | solution.py:40
  349.3 0.0 all-gather.14.cloned.1.call-update
  349.3 108.0 %all-gather.14.cloned.1.call-done = bf16[8192,1024]{1,0:T(8,128)(2,1)} async-done(((bf16[512,1024]{1,0:T(8,128)(2,1)}), bf16[8192,1024]{1,0:T(8,128)(2,1)}) %all-gather.14.cloned.1.call-update) | async-done | bytes 16777232 | tf_op jit(solution)/shard_map/all_gather | solution.py:44
  457.4 15.7 %multiply_subtract_fusion = f32[512,1024]{1,0:T(8,128)} fusion(bf16[512,8192]{1,0:T(8,128)(2,1)} %all-gather.10.cloned.1.call-done, bf16[8192,1024]{1,0:T(8,128)(2,1)} %all-gather.14.cloned.1.call-done, bf16[64,8,8,128]{3,2,1,0:T(8,128)(2,1)S(1)} %bitcast.30), kind=kOutput, calls=%fused_computation.2 | convolution fusion | flops 8591507456 | bytes 28311552 | tf_op jit(solution)/shard_map/dot_general | solution.py:40
  (5 shorter events, 0.0 us)
Async XLA Ops:
  6.5 116.1 %all-gather.8.cloned.1.call-start = ((), (), s32[]{:S(2)}) async-start(), calls=%async_computation | async-start | bytes 17825792 | tf_op jit(solution)/shard_map/all_gather | solution.py:20
  9.4 212.7 %all-gather.10.cloned.1.call-start = ((), (), s32[]{:S(2)}) async-start(), calls=%async_computation.1 | async-start | bytes 9437184 | tf_op jit(solution)/shard_map/all_gather | solution.py:36
  132.6 201.2 %all-gather.12.cloned.1.call-start = ((), (), s32[]{:S(2)}) async-start(), calls=%async_computation.2 | async-start | bytes 17825792 | tf_op jit(solution)/shard_map/all_gather | solution.py:42
  133.3 324.1 %all-gather.14.cloned.1.call-start = ((), (), s32[]{:S(2)}) async-start(), calls=%async_computation.3 | async-start | bytes 17825792 | tf_op jit(solution)/shard_map/all_gather | solution.py:44
Sparse Core Ops, SparseCore 0:
  9.8 112.8 all-gather.7
  132.7 89.4 all-gather.9
  224.6 109.1 all-gather.11
  349.5 107.8 all-gather.13
where the time goes:
time: 481 us; the launch traced here: 480 us
  waiting for transfers between devices  402 us (84%)
  matrix products  39.9 us (8%)
  blocking collectives  15.3 us (3%)
  between operations  14.4 us (3%)
  local copies, waits for them, and re-layouts  7.72 us (2%)
    all_gather x1, waiting for transfers between devices, local(): square = add_left(lax.all_gather(matrix, 'row', axis=0, tiled=True))  112 us
    all_gather x1, waiting for transfers between devices, local(): product = add_left(lax.all_gather(half_square, 'row', axis=0, tiled=True))  108 us
    all_gather x1, waiting for transfers between devices, local(): lax.all_gather(flattened, 'row', axis=0, tiled=True)  92.9 us
    all_gather x1, waiting for transfers between devices, local(): row_strip = lax.all_gather(matrix, 'col', axis=1, tiled=True)  88.8 us
    dot_general x2, matrix products, add_left(): return jnp.dot(row_strip, shard_piece, preferred_element_type=jnp.float32)  31.3 us
    all_gather x1, blocking collectives, local(): lax.all_gather(column_ids, 'row', axis=0, tiled=True)  15.3 us
  transfers between devices with their start and end apart: 4, of which 4 were waited for; matrix products, arithmetic and copies ran while one was open for 1% of the time, Pallas kernels for 0%

commit v1 on v0

v1 whole, which is shorter than its diff:
```python
import functools

import jax
import jax.numpy as jnp
from jax import lax
from jax.experimental import pallas as pl
from jax.experimental.pallas import tpu as pltpu
from jax.sharding import PartitionSpec as P

BLOCK = 128
BR = 4
BC = 8
CAP = 2
META = 16
NONE = 64


def pack_kernel(atom, column, count, blocks, send, seen, place):
    groups = send.shape[0]
    slots = blocks.shape[0]
    send[...] = jnp.zeros_like(send)
    for group in range(groups):
        seen[group] = 0
        for turn in range(CAP):
            place[group * CAP + turn] = NONE

    @pl.loop(0, slots)
    def _(slot):
        @pl.when(slot < count[0, 0])
        def _():
            group = atom[slot] // BR
            turn = jnp.minimum(seen[group], CAP - 1)
            seen[group] = turn + 1
            place[group * CAP + turn] = atom[slot] % BR * BC + column[slot]
            start = pl.multiple_of(turn * BLOCK, BLOCK)
            send[group, pl.ds(start, BLOCK), :] = blocks[slot]

    row = lax.broadcasted_iota(jnp.int32, (META, BLOCK), 0)
    for group in range(groups):
        value = jnp.where(row == 0, place[group * CAP], place[group * CAP + 1])
        send[group, CAP * BLOCK :, :] = value.astype(jnp.float32).astype(send.dtype)


def unpack_kernel(received, tile, place_vector, place, sem):
    owners = received.shape[0]
    tile[...] = jnp.zeros_like(tile)
    lane = lax.broadcasted_iota(jnp.int32, (META, BLOCK), 1)
    places = jnp.full((META, BLOCK), NONE, jnp.int32)
    for owner in range(owners):
        value = received[owner, CAP * BLOCK :, :].astype(jnp.float32).astype(jnp.int32)
        places = jnp.where(lane == owner, value, places)
    place_vector[...] = places
    copy = pltpu.make_async_copy(place_vector, place, sem)
    copy.start()
    copy.wait()

    @pl.loop(0, owners)
    def _(owner):
        for turn in range(CAP):
            at = place[turn, owner]

            @pl.when(at < BR * BC)
            def _():
                top = pl.multiple_of(at // BC * BLOCK, BLOCK)
                left = pl.multiple_of(at % BC * BLOCK, BLOCK)
                block = received[owner, turn * BLOCK : (turn + 1) * BLOCK, :]
                tile[pl.ds(top, BLOCK), pl.ds(left, BLOCK)] = block


def local_tile(blocks, block_atom, block_col, block_count):
    owners = lax.axis_size("row")
    vmem = pl.BlockSpec(memory_space=pltpu.VMEM)
    smem = pl.BlockSpec(memory_space=pltpu.SMEM)
    send = pl.pallas_call(
        pack_kernel,
        out_shape=jax.ShapeDtypeStruct((owners, CAP * BLOCK + META, BLOCK), blocks.dtype),
        in_specs=[smem, smem, smem, vmem],
        out_specs=vmem,
        scratch_shapes=[pltpu.SMEM((owners,), jnp.int32), pltpu.SMEM((owners * CAP,), jnp.int32)],
        compiler_params=pltpu.CompilerParams(vmem_limit_bytes=16 << 20),
        name="pack",
    )(block_atom[:, 0], block_col[:, 0], block_count, blocks)
    received = lax.all_to_all(send, "row", 0, 0, tiled=True)
    return pl.pallas_call(
        unpack_kernel,
        out_shape=jax.ShapeDtypeStruct((BR * BLOCK, BC * BLOCK), blocks.dtype),
        in_specs=[vmem],
        out_specs=vmem,
        scratch_shapes=[
            pltpu.VMEM((META, BLOCK), jnp.int32),
            pltpu.SMEM((META, BLOCK), jnp.int32),
            pltpu.SemaphoreType.DMA,
        ],
        compiler_params=pltpu.CompilerParams(vmem_limit_bytes=16 << 20),
        name="unpack",
    )(received)


def local(blocks, block_atom, block_col, block_count):
    matrix = local_tile(blocks, block_atom, block_col, block_count)
    row_strip = lax.all_gather(matrix, "col", axis=1, tiled=True)
    column_strip = lax.all_gather(matrix, "row", axis=0, tiled=True)
    factor = 0.5 / row_strip.shape[1]
    square = jnp.dot(row_strip, column_strip, preferred_element_type=jnp.float32)
    half_square = (square * factor).astype(jnp.bfloat16)
    half_strip = lax.all_gather(half_square, "col", axis=1, tiled=True)
    product = jnp.dot(half_strip, column_strip, preferred_element_type=jnp.float32)
    return 1.5 * matrix.astype(jnp.float32) - product


def solution(mesh):
    placed = (P("row", "col", None), P("row", "col"), P("row", "col"), P("row", "col"))
    return jax.shard_map(
        local, mesh=mesh, in_specs=placed, out_specs=P("row", "col"), check_vma=False
    )
```

time: 481 us -> 370 us (0.77)
  waiting for transfers between devices: 402 us -> 291 us
  blocking collectives: 15.3 us -> 26.2 us
  matrix products: 39.9 us -> 31.4 us
  local copies, waits for them, and re-layouts: 7.72 us -> 2.53 us
    all_gather x3 -> x2, waiting for transfers between devices: 313 us -> 201 us  [the longest x1 112 us: local(): column_strip = lax.all_gather(matrix, 'row', axis=0, tiled=True)]
    all_to_all x0 -> x1, blocking collectives: none -> 26.2 us  [local_tile(): received = lax.all_to_all(send, 'row', 0, 0, tiled=True)]
    all_gather x1 -> x0, blocking collectives: 15.3 us -> none  [local(): lax.all_gather(column_ids, 'row', axis=0, tiled=True)]
    dot_general x3 -> x2, matrix products: 39.9 us -> 31.4 us  [the longest x1 15.9 us: local(): jnp.dot(half_strip, column_strip, preferred_element_type=jnp.float32)]
    unnamed x7 -> x6, local copies, waits for them, and re-layouts: 7.56 us -> 2.53 us
  transfers between devices with their start and end apart: 4 -> 3, of which waited for: 4 -> 3; matrix products, arithmetic and copies ran while one was open for 1% -> 0% of each run, Pallas kernels for 0% -> 0%
where the time goes in v1:
time: 370 us; the launch traced here: 369 us
  waiting for transfers between devices  291 us (79%)
  matrix products  31.4 us (8%)
  blocking collectives  26.2 us (7%)
  between operations  13.8 us (4%)
  Pallas kernels  4.01 us (1%)
    all_gather x1, waiting for transfers between devices, local(): column_strip = lax.all_gather(matrix, 'row', axis=0, tiled=True)  112 us
    all_gather x1, waiting for transfers between devices, local(): half_strip = lax.all_gather(half_square, 'col', axis=1, tiled=True)  89.6 us
    all_gather x1, waiting for transfers between devices, local(): row_strip = lax.all_gather(matrix, 'col', axis=1, tiled=True)  88.9 us
    all_to_all x1, blocking collectives, local_tile(): received = lax.all_to_all(send, 'row', 0, 0, tiled=True)  26.2 us
    dot_general x1, matrix products, local(): jnp.dot(half_strip, column_strip, preferred_element_type=jnp.float32)  15.9 us
    dot_general x1, matrix products, local(): jnp.dot(row_strip, column_strip, preferred_element_type=jnp.float32)  15.5 us
  transfers between devices with their start and end apart: 3, of which 3 were waited for; matrix products, arithmetic and copies ran while one was open for 0% of the time, Pallas kernels for 0%

profile of v1, /device:TPU:0, one launch (start us, length us, event | category | flops | bytes accessed | tf_op | source)
XLA Modules:
  0.0 368.9 jit_solution(5218661739044760200)
XLA Ops:
  6.5 0.0 all-gather.4.cloned.1.call-start
  7.2 0.0 copy-start
  7.2 1.2 copy-done
  8.4 0.0 copy-start.1
  8.4 0.7 copy-done.1
  9.1 0.0 copy-start.2
  9.1 0.7 copy-done.2
  9.7 1.7 pack.1
  11.4 26.2 %all_to_all.5.received = bf16[16,272,128]{2,1,0:T(8,128)(2,1)S(1)} all-to-all(bf16[16,272,128]{2,1,0:T(8,128)(2,1)S(1)} %pack.1), channel_id=1, replica_groups=mesh['row'=16,'col'=8] {'row'}, dimensions={0} | all-to-all | bytes 2228224 | tf_op jit(solution)/shard_map/all_to_all | solution.py:83
  37.6 2.4 unpack.1
  40.0 0.0 all-gather.4.cloned.1.call-update
  40.0 0.0 all-gather.6.cloned.1.call-start
  40.0 0.7 all-gather.6.cloned.1.call-update
  40.7 0.0 all-gather.8.cloned.1.call-start
  40.8 88.9 %all-gather.4.cloned.1.call-done = bf16[512,8192]{1,0:T(8,128)(2,1)} async-done(((bf16[512,1024]{1,0:T(8,128)(2,1)}), bf16[512,8192]{1,0:T(8,128)(2,1)}) %all-gather.4.cloned.1.call-update) | async-done | bytes 8388624 | tf_op jit(solution)/shard_map/all_gather | solution.py:101
  129.7 111.6 %all-gather.6.cloned.1.call-done = bf16[8192,1024]{1,0:T(8,128)(2,1)} async-done(((bf16[512,1024]{1,0:T(8,128)(2,1)}), bf16[8192,1024]{1,0:T(8,128)(2,1)}) %all-gather.6.cloned.1.call-update) | async-done | bytes 16777232 | tf_op jit(solution)/shard_map/all_gather | solution.py:102
  241.3 15.5 %multiply_convert_fusion = bf16[512,1024]{1,0:T(8,128)(2,1)} fusion(bf16[512,8192]{1,0:T(8,128)(2,1)} %all-gather.4.cloned.1.call-done, bf16[8192,1024]{1,0:T(8,128)(2,1)} %all-gather.6.cloned.1.call-done), kind=kOutput, calls=%fused_computation | convolution fusion | flops 8590983168 | bytes 26214400 | tf_op jit(solution)/shard_map/dot_general | solution.py:104
  256.9 0.0 all-gather.8.cloned.1.call-update
  256.9 89.6 %all-gather.8.cloned.1.call-done = bf16[512,8192]{1,0:T(8,128)(2,1)} async-done(((bf16[512,1024]{1,0:T(8,128)(2,1)}), bf16[512,8192]{1,0:T(8,128)(2,1)}) %all-gather.8.cloned.1.call-update) | async-done | bytes 8388624 | tf_op jit(solution)/shard_map/all_gather | solution.py:106
  346.5 15.9 %multiply_subtract_fusion = f32[512,1024]{1,0:T(8,128)} fusion(bf16[512,1024]{1,0:T(8,128)(2,1)} %unpack.1, bf16[512,8192]{1,0:T(8,128)(2,1)} %all-gather.8.cloned.1.call-done, bf16[8192,1024]{1,0:T(8,128)(2,1)} %all-gather.6.cloned.1.call-done), kind=kOutput, calls=%fused_computation.1 | convolution fusion | flops 8591507456 | bytes 28311552 | tf_op jit(solution)/shard_map/dot_general | solution.py:107
Async XLA Ops:
  6.5 123.2 %all-gather.4.cloned.1.call-start = ((), (), s32[]{:S(2)}) async-start(), calls=%async_computation.1 | async-start | bytes 9437184 | tf_op jit(solution)/shard_map/all_gather | solution.py:101
  7.2 1.2 copy-start
  8.4 0.7 copy-start.1
  9.1 0.7 copy-start.2
  40.0 201.3 %all-gather.6.cloned.1.call-start = ((), (), s32[]{:S(2)}) async-start(), calls=%async_computation.2 | async-start | bytes 17825792 | tf_op jit(solution)/shard_map/all_gather | solution.py:102
  40.7 305.8 %all-gather.8.cloned.1.call-start = ((), (), s32[]{:S(2)}) async-start(), calls=%async_computation.3 | async-start | bytes 9437184 | tf_op jit(solution)/shard_map/all_gather | solution.py:106
Sparse Core Ops, SparseCore 0:
  40.1 89.5 all-gather.3
  132.2 109.1 all-gather.5
  257.0 89.4 all-gather.7

commit v2 on v1

--- a/solution.py
+++ b/solution.py
@@ -96,16 +96,248 @@
     )(received)
 
 
+def product_kernel(factor, left_parts, right_rows, first_row, has_base, left_at, right_at, *refs):
+    lefts, refs = refs[: len(left_parts)], refs[len(left_parts) :]
+    pieces_total = sum(map(len, right_rows))
+    rights, refs = refs[:pieces_total], refs[pieces_total:]
+    if has_base:
+        base, refs = refs[0], refs[1:]
+    out, held, staged, total, left_sems, right_sems = refs
+    depth = staged.shape[1]
+    copies = []
+    for index, (left, (source, first, count)) in enumerate(zip(lefts, left_parts)):
+        for side in range(2):
+            copy = pltpu.make_async_copy(
+                left.at[pl.ds(source, count), pl.ds(side * depth, depth)],
+                held.at[left_at[index] * 2 + side, pl.ds(first, count)],
+                left_sems.at[index, side],
+            )
+            copy.start()
+            copies.append(copy)
+    slots = staged.shape[0]
+    loads, at = [], 0
+    for index, pieces in enumerate(right_rows):
+        load = []
+        for part, (first, count) in enumerate(pieces):
+            load.append(
+                pltpu.make_async_copy(
+                    rights[at],
+                    staged.at[index % slots, pl.ds(first, count)],
+                    right_sems.at[index % slots, part],
+                )
+            )
+            at += 1
+        loads.append(load)
+    for load in loads[: slots - 1]:
+        for copy in load:
+            copy.start()
+    for copy in copies:
+        copy.wait()
+    for index in range(len(loads)):
+        ahead = index + slots - 1
+        if ahead < len(loads):
+            for copy in loads[ahead]:
+                copy.start()
+        for copy in loads[index]:
+            copy.wait()
+        term = jnp.dot(
+            held[right_at[index]], staged[index % slots], preferred_element_type=jnp.float32
+        )
+        if index == 0:
+            total[...] = term
+        elif index < len(loads) - 1:
+            total[...] += term
+        else:
+            value = (total[...] + term) * factor
+            if has_base:
+                value = 1.5 * base[...].astype(jnp.float32) - value
+            out[...] = value.astype(out.dtype)
+
+
+def product(lefts, rights, rows, factor, dtype, name, base=None):
+    width = lefts[0][0].shape[1]
+    right_arrays = [array for _, pieces in rights for array, _ in pieces]
+    columns = right_arrays[0].shape[1]
+    depth = width // 2
+    left_parts = [(source, first, count) for _, _, source, first, count in lefts]
+    right_rows = [[(first, array.shape[0]) for array, first in pieces] for _, pieces in rights]
+    left_at = jnp.stack([part[1] for part in lefts]).astype(jnp.int32)
+    right_at = jnp.stack([chunk for chunk, _ in rights]).astype(jnp.int32)
+    smem = pl.BlockSpec(memory_space=pltpu.SMEM)
+    vmem = pl.BlockSpec(memory_space=pltpu.VMEM)
+    hbm = pl.BlockSpec(memory_space=pltpu.HBM)
+    operands = [left_at, right_at] + [part[0] for part in lefts] + right_arrays
+    specs = [smem, smem] + [hbm] * (len(operands) - 2)
+    if base is not None:
+        operands.append(base)
+        specs.append(vmem)
+    slots = 4
+    return pl.pallas_call(
+        functools.partial(product_kernel, factor, left_parts, right_rows, 0, base is not None),
+        out_shape=jax.ShapeDtypeStruct((rows, columns), dtype),
+        in_specs=specs,
+        out_specs=vmem,
+        scratch_shapes=[
+            pltpu.VMEM((len(rights), rows, depth), lefts[0][0].dtype),
+            pltpu.VMEM((slots, depth, columns), lefts[0][0].dtype),
+            pltpu.VMEM((rows, columns), jnp.float32),
+            pltpu.SemaphoreType.DMA((len(lefts), 2)),
+            pltpu.SemaphoreType.DMA((slots, 2)),
+        ],
+        compiler_params=pltpu.CompilerParams(vmem_limit_bytes=48 << 20),
+        cost_estimate=pl.CostEstimate(
+            flops=2 * rows * columns * depth * len(rights),
+            bytes_accessed=2 * depth * len(rights) * (rows + columns),
+            transcendentals=0,
+        ),
+        name=name,
+    )(*operands)
+
+
+def over_row(value, z_step, y_step, core_step):
+    size = lax.axis_size("row")
+    pairs = []
+    for source in range(size):
+        z, y, core = source // 8, source // 2 % 4, source % 2
+        target = ((z + z_step) % 2 * 4 + (y + y_step) % 4) * 2 + (core + core_step) % 2
+        pairs.append((source, target))
+    return lax.ppermute(value, "row", pairs)
+
+
+def over_col(value, z_step, x_step):
+    size = lax.axis_size("col")
+    pairs = []
+    for source in range(size):
+        z, x = source // 4, source % 4
+        pairs.append((source, (z + z_step) % 2 * 4 + (x + x_step) % 4))
+    return lax.ppermute(value, "col", pairs)
+
+
+def x_shift(value, step):
+    return over_col(value, 0, step)
+
+
+def y_shift(value, step):
+    return over_row(value, 0, step, 0)
+
+
+def z_swap(value):
+    return over_col(value, 1, 0)
+
+
+def core_swap(value):
+    return over_row(value, 0, 0, 1)
+
+
+def after(values, *earlier):
+    return lax.optimization_barrier((values, earlier))[0]
+
+
+def near(value, shift):
+    return shift(value, 1), shift(value, -1)
+
+
+def far(below, above, shift):
+    half = below.shape[0] // 2
+    return shift(below[:half], 1), shift(above[half:], -1)
+
+
 def local(blocks, block_atom, block_col, block_count):
     matrix = local_tile(blocks, block_atom, block_col, block_count)
-    row_strip = lax.all_gather(matrix, "col", axis=1, tiled=True)
-    column_strip = lax.all_gather(matrix, "row", axis=0, tiled=True)
-    factor = 0.5 / row_strip.shape[1]
-    square = jnp.dot(row_strip, column_strip, preferred_element_type=jnp.float32)
-    half_square = (square * factor).astype(jnp.bfloat16)
-    half_strip = lax.all_gather(half_square, "col", axis=1, tiled=True)
-    product = jnp.dot(half_strip, column_strip, preferred_element_type=jnp.float32)
-    return 1.5 * matrix.astype(jnp.float32) - product
+    rows = matrix.shape[0]
+    half = rows // 2
+    quarter = half // 2
+    row, col = lax.axis_index("row"), lax.axis_index("col")
+    z_hi, y, core = row // 8, row // 2 % 4, row % 2
+    z_lo, x = col // 4, col % 4
+
+    def col_chunk(z_step, x_step):
+        return (z_lo + z_step) % 2 * 4 + (x + x_step) % 4
+
+    def row_chunk(z_step, y_step, core_step):
+        return ((z_hi + z_step) % 2 * 4 + (y + y_step) % 4) * 2 + (core + core_step) % 2
+
+    top, bottom = matrix[:half], matrix[half:]
+    other_z = over_row(matrix, 1, 0, 0)
+    x_near = near(matrix, x_shift)
+    y_near = near(matrix, y_shift)
+    top, bottom, matrix_b, other_z, x_near, y_near = after((top, bottom, matrix, other_z, x_near, y_near))
+    top_z = z_swap(top)
+    x_far = far(*x_near, x_shift)
+    y_far = far(*y_near, y_shift)
+    z_near = near(other_z, y_shift)
+    swapped = {}
+    swapped["own"] = core_swap(matrix_b)
+    swapped["near"] = [core_swap(v) for v in y_near]
+    bottom, top_z, x_far = after((bottom, top_z, x_far))
+    bottom_z = z_swap(bottom)
+    top_z_near = near(top_z, x_shift)
+    bottom_z, top_z_near = after((bottom_z, top_z_near))
+    top_z_far = far(*top_z_near, x_shift)
+    bottom_z_near = near(bottom_z, x_shift)
+    z_near, y_far, top_z_far, other_z_b = after((z_near, y_far, top_z_far, other_z))
+    z_far = far(*z_near, y_shift)
+    swapped["far"] = [core_swap(v) for v in y_far]
+    swapped["z"] = core_swap(other_z_b)
+    swapped["z near"] = [core_swap(v) for v in z_near]
+    bottom_z_near, z_far_b = after((bottom_z_near, z_far))
+    bottom_z_far = far(*bottom_z_near, x_shift)
+    z_far = z_far_b
+    swapped["z far"] = [core_swap(v) for v in z_far]
+
+    pieces = [
+        (0, 0, [(matrix, 0)], [(swapped["own"], 0)]),
+        (0, -1, [(y_near[0], 0)], [(swapped["near"][0], 0)]),
+        (0, 1, [(y_near[1], 0)], [(swapped["near"][1], 0)]),
+        (0, 2, [(y_far[0], 0), (y_far[1], half)], [(swapped["far"][0], 0), (swapped["far"][1], half)]),
+        (1, 0, [(other_z, 0)], [(swapped["z"], 0)]),
+        (1, -1, [(z_near[0], 0)], [(swapped["z near"][0], 0)]),
+        (1, 1, [(z_near[1], 0)], [(swapped["z near"][1], 0)]),
+        (1, 2, [(z_far[0], 0), (z_far[1], half)], [(swapped["z far"][0], 0), (swapped["z far"][1], half)]),
+    ]
+    chunks = []
+    for z_step, y_step, mine, others in pieces:
+        chunks.append((row_chunk(z_step, y_step, 0), mine))
+        chunks.append((row_chunk(z_step, y_step, 1), others))
+
+    def strip(z_step, own, near_two, far_two, source=0):
+        return [
+            (own, col_chunk(z_step, 0), source, 0, half),
+            (near_two[0], col_chunk(z_step, -1), source, 0, half),
+            (near_two[1], col_chunk(z_step, 1), source, 0, half),
+            (far_two[0], col_chunk(z_step, 2), 0, 0, quarter),
+            (far_two[1], col_chunk(z_step, 2), 0, quarter, quarter),
+        ]
+
+    def own_strip(source, far_one):
+        return strip(0, matrix, x_near, x_far, source)[:3] + [(far_one, col_chunk(0, 2), 0, 0, half)]
+
+    factor = 0.5 / (matrix.shape[1] * lax.axis_size("col"))
+    kind = matrix.dtype
+    lefts = own_strip(0, x_far[0]) + strip(1, top_z, top_z_near, top_z_far)
+    half_top = product(lefts, chunks, half, factor, kind, "square_top")
+    top_near = near(half_top, x_shift)
+    top_swapped = z_swap(half_top)
+    bottom_z, bottom_z_near, bottom_z_far = after((bottom_z, bottom_z_near, bottom_z_far), half_top)
+    lefts = own_strip(half, x_far[1]) + strip(1, bottom_z, bottom_z_near, bottom_z_far)
+    half_bottom = product(lefts, chunks, half, factor, kind, "square_bottom")
+    bottom_swapped = z_swap(half_bottom)
+    bottom_near = near(half_bottom, x_shift)
+    top_near, half_bottom = after((top_near, half_bottom))
+    top_far = far(*top_near, x_shift)
+    top_swapped_near = [z_swap(v) for v in top_near]
+    bottom_near, bottom_swapped, top_far, top_swapped = after((bottom_near, bottom_swapped, top_far, top_swapped))
+    bottom_far = far(*bottom_near, x_shift)
+    bottom_swapped_near = near(bottom_swapped, x_shift)
+    top_swapped_far = [z_swap(v) for v in top_far]
+    bottom_swapped_near = after(bottom_swapped_near, bottom_far)
+    bottom_swapped_far = far(*bottom_swapped_near, x_shift)
+    lefts = strip(0, half_top, top_near, top_far) + strip(1, top_swapped, top_swapped_near, top_swapped_far)
+    out_top = product(lefts, chunks, half, 1.0, jnp.float32, "step_top", top)
+    lefts = strip(0, half_bottom, bottom_near, bottom_far)
+    lefts += strip(1, bottom_swapped, bottom_swapped_near, bottom_swapped_far)
+    out_bottom = product(lefts, chunks, half, 1.0, jnp.float32, "step_bottom", matrix[half:])
+    return jnp.concatenate([out_top, out_bottom], axis=0)
 
 
 def solution(mesh):

time: 370 us -> 254 us (0.69)
  waiting for transfers between devices: 291 us -> 102 us
  starting transfers between devices: 0.08 us -> 58.2 us
  Pallas kernels: 4.01 us -> 41.8 us
  matrix products: 31.4 us -> 0 us
  local copies, waits for them, and re-layouts: 2.53 us -> 19.5 us
  between operations: 13.8 us -> 1.49 us
    all_gather x3 -> x0, waiting for transfers between devices: 290 us -> none  [the longest x1 112 us: local(): column_strip = lax.all_gather(matrix, 'row', axis=0, tiled=True)]
    ppermute x0 -> x51, waiting for transfers between devices: none -> 102 us  [the longest x32 62.9 us: over_col(): return lax.ppermute(value, 'col', pairs)]
    ppermute x0 -> x51, starting transfers between devices: none -> 58.2 us  [the longest x32 43 us: over_col(): return lax.ppermute(value, 'col', pairs)]
    pallas_call x0 -> x4, Pallas kernels: none -> 39.2 us  [product(): pl.pallas_call(functools.partial(product_kernel, factor, left_parts, righ...]
    dot_general x2 -> x0, matrix products: 31.4 us -> none  [the longest x1 15.9 us: local(): jnp.dot(half_strip, column_strip, preferred_element_type=jnp.float32)]
    unnamed x6 -> x84, local copies, waits for them, and re-layouts: 2.53 us -> 11.7 us
    slice x0 -> x17, local copies, waits for them, and re-layouts: none -> 7.52 us  [the longest x16 7.45 us: far(): return (shift(below[:half], 1), shift(above[half:], -1))]
  transfers between devices with their start and end apart: 3 -> 51, of which waited for: 3 -> 22; matrix products, arithmetic and copies ran while one was open for 0% -> 3% of each run, Pallas kernels for 0% -> 11%
where the time goes in v2:
time: 254 us; the launch traced here: 252 us
  waiting for transfers between devices  102 us (40%)
  starting transfers between devices  58.2 us (23%)
  Pallas kernels  41.8 us (16%)
  blocking collectives  26.5 us (10%)
  local copies, waits for them, and re-layouts  19.5 us (8%)
  other arithmetic  2.79 us (1%)
    ppermute x32, waiting for transfers between devices, over_col(): return lax.ppermute(value, 'col', pairs)  62.9 us
    ppermute x32, starting transfers between devices, over_col(): return lax.ppermute(value, 'col', pairs)  43 us
    pallas_call x4, Pallas kernels, product(): pl.pallas_call(functools.partial(product_kernel, factor, left_parts, righ...  39.2 us
    ppermute x19, waiting for transfers between devices, over_row(): return lax.ppermute(value, 'row', pairs)  39.1 us
    all_to_all x1, blocking collectives, local_tile(): received = lax.all_to_all(send, 'row', 0, 0, tiled=True)  26.5 us
    ppermute x19, starting transfers between devices, over_row(): return lax.ppermute(value, 'row', pairs)  15.2 us
    unnamed x84, local copies, waits for them, and re-layouts  11.7 us
    slice x16, local copies, waits for them, and re-layouts, far(): return (shift(below[:half], 1), shift(above[half:], -1))  7.45 us
  transfers between devices with their start and end apart: 51, of which 22 were waited for; matrix products, arithmetic and copies ran while one was open for 3% of the time, Pallas kernels for 11%

profile of v2, /device:TPU:0, one launch (start us, length us, event | category | flops | bytes accessed | tf_op | source)
XLA Modules:
  0.0 252.4 jit_solution(8159865206394174712)
XLA Ops:
  4.5 26.5 %all_to_all.5.received = bf16[16,272,128]{2,1,0:T(8,128)(2,1)S(1)} all-to-all(bf16[16,272,128]{2,1,0:T(8,128)(2,1)S(1)} %pack.1), channel_id=1, replica_groups=mesh['row'=16,'col'=8] {'row'}, dimensions={0} | all-to-all | bytes 2228224 | tf_op jit(solution)/shard_map/all_to_all | solution.py:83
  36.9 2.7 %collective-permute-start.4 = (bf16[512,1024]{1,0:T(8,128)(2,1)S(1)}, bf16[512,1024]{1,0:T(8,128)(2,1)S(1)}, u32[]{:S(2)}, u32[]{:S(2)}) collective-permute-start(bf16[512,1024]{1,0:T(8,128)(2,1)S(1)} %unpack.1.refs_0_.refs_9_.refs_10_), channel_id=1, source_target_pairs={{0,48},{8,56},{16,0},{24,8},{32,16},{40,24},{48,32},{56,40},{64,11... | collective-permute-start | bytes 3145736 | tf_op jit(solution)/shard_map/ppermute | solution.py:204
  39.7 19.5 %collective-permute-done.refs_19_.refs_20_ = bf16[512,1024]{1,0:T(8,128)(2,1)} collective-permute-done((bf16[512,1024]{1,0:T(8,128)(2,1)S(1)}, bf16[512,1024]{1,0:T(8,128)(2,1)}, u32[]{:S(2)}, u32[]{:S(2)}) %collective-permute-start) | collective-permute-done | bytes 1048608 | tf_op jit(solution)/shard_map/ppermute | solution.py:204
  59.2 2.6 %collective-permute-done.3.refs_11_.refs_12_ = bf16[512,1024]{1,0:T(8,128)(2,1)S(1)} collective-permute-done((bf16[512,1024]{1,0:T(8,128)(2,1)S(1)}, bf16[512,1024]{1,0:T(8,128)(2,1)S(1)}, u32[]{:S(2)}, u32[]{:S(2)}) %collective-permute-start.3) | collective-permute-done | bytes 1048608 | tf_op jit(solution)/shard_map/ppermute | solution.py:204
  62.3 3.0 %collective-permute-start.7 = (bf16[256,1024]{1,0:T(8,128)(2,1)S(1)}, bf16[256,1024]{1,0:T(8,128)(2,1)S(1)}, u32[]{:S(2)}, u32[]{:S(2)}) collective-permute-start(bf16[256,1024]{1,0:T(8,128)(2,1)S(1)} %slice.58), channel_id=1, source_target_pairs={{0,3},{1,0},{2,1},{3,2},{4,7},{5,4},{6,5},{7,6},{8,11},{9,8},{10,9... | collective-permute-start | bytes 1572872 | tf_op jit(solution)/shard_map/ppermute | solution.py:213
  66.6 3.3 %collective-permute-start.14 = (bf16[256,1024]{1,0:T(8,128)(2,1)S(1)}, bf16[256,1024]{1,0:T(8,128)(2,1)S(1)}, u32[]{:S(2)}, u32[]{:S(2)}) collective-permute-start(bf16[256,1024]{1,0:T(8,128)(2,1)S(1)} %slice.60), channel_id=1, source_target_pairs={{0,48},{8,56},{16,0},{24,8},{32,16},{40,24},{48,32},{56,40},{64,11... | collective-permute-start | bytes 1572872 | tf_op jit(solution)/shard_map/ppermute | solution.py:204
  69.9 5.3 %collective-permute-done.6.refs_3_ = bf16[256,1024]{1,0:T(8,128)(2,1)S(1)} collective-permute-done((bf16[256,1024]{1,0:T(8,128)(2,1)S(1)}, bf16[256,1024]{1,0:T(8,128)(2,1)S(1)}, u32[]{:S(2)}, u32[]{:S(2)}) %collective-permute-start.6) | collective-permute-done | bytes 524320 | tf_op jit(solution)/shard_map/ppermute | solution.py:213
  76.8 2.3 collective-permute-start.10
  79.2 3.1 %collective-permute-start.12 = (bf16[512,1024]{1,0:T(8,128)(2,1)}, bf16[512,1024]{1,0:T(8,128)(2,1)}, u32[]{:S(2)}, u32[]{:S(2)}) collective-permute-start(bf16[512,1024]{1,0:T(8,128)(2,1)} %collective-permute-done.refs_19_.refs_20_), channel_id=1, source_target_pairs={{0,48},{8,56},{16,0},{24,8},{32,16},{40,24},{48,32},{56,40},{64,11... | collective-permute-start | bytes 3145736 | tf_op jit(solution)/shard_map/ppermute | solution.py:204
  83.7 4.3 %collective-permute-done.10.refs_6_ = bf16[256,1024]{1,0:T(8,128)(2,1)S(1)} collective-permute-done((bf16[256,1024]{1,0:T(8,128)(2,1)S(1)}, bf16[256,1024]{1,0:T(8,128)(2,1)S(1)}, u32[]{:S(2)}, u32[]{:S(2)}) %collective-permute-start.10) | collective-permute-done | bytes 524320 | tf_op jit(solution)/shard_map/ppermute | solution.py:213
  87.9 2.9 %collective-permute-done.9.refs_5_ = bf16[256,1024]{1,0:T(8,128)(2,1)S(1)} collective-permute-done((bf16[256,1024]{1,0:T(8,128)(2,1)S(1)}, bf16[256,1024]{1,0:T(8,128)(2,1)S(1)}, u32[]{:S(2)}, u32[]{:S(2)}) %collective-permute-start.9) | collective-permute-done | bytes 524320 | tf_op jit(solution)/shard_map/ppermute | solution.py:213
  92.3 10.0 %collective-permute-done.11.refs_21_.refs_22_ = bf16[512,1024]{1,0:T(8,128)(2,1)} collective-permute-done((bf16[512,1024]{1,0:T(8,128)(2,1)}, bf16[512,1024]{1,0:T(8,128)(2,1)}, u32[]{:S(2)}, u32[]{:S(2)}) %collective-permute-start.11) | collective-permute-done | bytes 1048608 | tf_op jit(solution)/shard_map/ppermute | solution.py:204
  102.5 3.3 %collective-permute-start.16 = (bf16[128,1024]{1,0:T(8,128)(2,1)S(1)}, bf16[128,1024]{1,0:T(8,128)(2,1)S(1)}, u32[]{:S(2)}, u32[]{:S(2)}) collective-permute-start(bf16[128,1024]{1,0:T(8,128)(2,1)S(1)} %slice.62), channel_id=1, source_target_pairs={{0,3},{1,0},{2,1},{3,2},{4,7},{5,4},{6,5},{7,6},{8,11},{9,8},{10,9... | collective-permute-start | bytes 786440 | tf_op jit(solution)/shard_map/ppermute | solution.py:213
  105.7 5.7 %collective-permute-done.15.refs_7_ = bf16[128,1024]{1,0:T(8,128)(2,1)S(1)} collective-permute-done((bf16[128,1024]{1,0:T(8,128)(2,1)S(1)}, bf16[128,1024]{1,0:T(8,128)(2,1)S(1)}, u32[]{:S(2)}, u32[]{:S(2)}) %collective-permute-start.15) | collective-permute-done | bytes 262176 | tf_op jit(solution)/shard_map/ppermute | solution.py:213
  111.5 3.6 %collective-permute-start.26 = (bf16[256,1024]{1,0:T(8,128)(2,1)S(1)}, bf16[256,1024]{1,0:T(8,128)(2,1)S(1)}, u32[]{:S(2)}, u32[]{:S(2)}) collective-permute-start(bf16[256,1024]{1,0:T(8,128)(2,1)S(1)} %collective-permute-done.8.refs_4_), channel_id=1, source_target_pairs={{0,3},{1,0},{2,1},{3,2},{4,7},{5,4},{6,5},{7,6},{8,11},{9,8},{10,9... | collective-permute-start | bytes 1572872 | tf_op jit(solution)/shard_map/ppermute | solution.py:213
  117.9 2.8 %collective-permute-start.28 = (bf16[256,1024]{1,0:T(8,128)(2,1)S(1)}, bf16[256,1024]{1,0:T(8,128)(2,1)}, u32[]{:S(2)}, u32[]{:S(2)}) collective-permute-start(bf16[256,1024]{1,0:T(8,128)(2,1)S(1)} %slice.64), channel_id=1, source_target_pairs={{0,48},{8,56},{16,0},{24,8},{32,16},{40,24},{48,32},{56,40},{64,11... | collective-permute-start | bytes 1572872 | tf_op jit(solution)/shard_map/ppermute | solution.py:204
  122.5 4.2 %collective-permute-done.27.refs_25_.refs_26_ = bf16[256,1024]{1,0:T(8,128)(2,1)S(1)} collective-permute-done((bf16[256,1024]{1,0:T(8,128)(2,1)S(1)}, bf16[256,1024]{1,0:T(8,128)(2,1)S(1)}, u32[]{:S(2)}, u32[]{:S(2)}) %collective-permute-start.27) | collective-permute-done | bytes 524320 | tf_op jit(solution)/shard_map/ppermute | solution.py:204
  138.3 8.7 %square_top.1.refs_0_ = bf16[256,1024]{1,0:T(8,128)(2,1)S(1)} custom-call(s32[9]{0:T(128)S(1)} %stack.80.left_at, s32[16]{0:T(128)S(1)} %stack.79.right_at, bf16[512,1024]{1,0:T(8,128)(2,1)} %copy-done, bf16[512,1024]{1,0:T(8,128)(2,1)} %copy-done.37, bf16[512,1024]{1,0:T(8,128)(2,1)} %copy-done.38, bf16[256,1024]{1,0:T(8,128)(2,1)S(1)} %copy-done.19, ...), custom_call_target="tpu_custom_call" | custom-call | flops 4294967296 | bytes 20971520 | tf_op jit(solution)/shard_map/square_top/pallas_call | solution.py:175
  147.6 2.8 %collective-permute-start.32 = (bf16[256,1024]{1,0:T(8,128)(2,1)S(1)}, bf16[256,1024]{1,0:T(8,128)(2,1)}, u32[]{:S(2)}, u32[]{:S(2)}) collective-permute-start(bf16[256,1024]{1,0:T(8,128)(2,1)S(1)} %square_top.1.refs_0_), channel_id=1, source_target_pairs={{0,3},{1,0},{2,1},{3,2},{4,7},{5,4},{6,5},{7,6},{8,11},{9,8},{10,9... | collective-permute-start | bytes 1572872 | tf_op jit(solution)/shard_map/ppermute | solution.py:213
  150.4 8.9 %square_bottom.1.refs_0_ = bf16[256,1024]{1,0:T(8,128)(2,1)S(1)} custom-call(s32[9]{0:T(128)S(1)} %stack.80.left_at, s32[16]{0:T(128)S(1)} %stack.79.right_at, bf16[512,1024]{1,0:T(8,128)(2,1)} %copy-done, bf16[512,1024]{1,0:T(8,128)(2,1)} %copy-done.37, bf16[512,1024]{1,0:T(8,128)(2,1)} %copy-done.38, bf16[256,1024]{1,0:T(8,128)(2,1)S(1)} %copy-done.17, ...), custom_call_target="tpu_custom_call" | custom-call | flops 4294967296 | bytes 20971520 | tf_op jit(solution)/shard_map/square_bottom/pallas_call | solution.py:175
  159.4 3.2 %collective-permute-start.36 = (bf16[256,1024]{1,0:T(8,128)(2,1)S(1)}, bf16[256,1024]{1,0:T(8,128)(2,1)S(1)}, u32[]{:S(2)}, u32[]{:S(2)}) collective-permute-start(bf16[256,1024]{1,0:T(8,128)(2,1)S(1)} %square_bottom.1.refs_0_), channel_id=1, source_target_pairs={{0,3},{1,0},{2,1},{3,2},{4,7},{5,4},{6,5},{7,6},{8,11},{9,8},{10,9... | collective-permute-start | bytes 1572872 | tf_op jit(solution)/shard_map/ppermute | solution.py:213
  166.7 8.7 %collective-permute-done.35.refs_1_ = bf16[256,1024]{1,0:T(8,128)(2,1)S(1)} collective-permute-done((bf16[256,1024]{1,0:T(8,128)(2,1)S(1)}, bf16[256,1024]{1,0:T(8,128)(2,1)S(1)}, u32[]{:S(2)}, u32[]{:S(2)}) %collective-permute-start.35) | collective-permute-done | bytes 524320 | tf_op jit(solution)/shard_map/ppermute | solution.py:213
  177.6 8.8 %collective-permute-done.40.refs_5_ = bf16[256,1024]{1,0:T(8,128)(2,1)S(1)} collective-permute-done((bf16[256,1024]{1,0:T(8,128)(2,1)S(1)}, bf16[256,1024]{1,0:T(8,128)(2,1)S(1)}, u32[]{:S(2)}, u32[]{:S(2)}) %collective-permute-start.40) | collective-permute-done | bytes 524320 | tf_op jit(solution)/shard_map/ppermute | solution.py:213
  188.1 3.3 %collective-permute-start.48 = (bf16[256,1024]{1,0:T(8,128)(2,1)}, bf16[256,1024]{1,0:T(8,128)(2,1)}, u32[]{:S(2)}, u32[]{:S(2)}) collective-permute-start(bf16[256,1024]{1,0:T(8,128)(2,1)} %collective-permute-done.37.refs_5_), channel_id=1, source_target_pairs={{0,3},{1,0},{2,1},{3,2},{4,7},{5,4},{6,5},{7,6},{8,11},{9,8},{10,9... | collective-permute-start | bytes 1572872 | tf_op jit(solution)/shard_map/ppermute | solution.py:213
  195.0 3.6 %collective-permute-done.45.refs_3_ = bf16[128,1024]{1,0:T(8,128)(2,1)S(1)} collective-permute-done((bf16[128,1024]{1,0:T(8,128)(2,1)S(1)}, bf16[128,1024]{1,0:T(8,128)(2,1)S(1)}, u32[]{:S(2)}, u32[]{:S(2)}) %collective-permute-start.45) | collective-permute-done | bytes 262176 | tf_op jit(solution)/shard_map/ppermute | solution.py:213
  200.1 6.0 %collective-permute-done.46.refs_4_ = bf16[128,1024]{1,0:T(8,128)(2,1)S(1)} collective-permute-done((bf16[128,1024]{1,0:T(8,128)(2,1)S(1)}, bf16[128,1024]{1,0:T(8,128)(2,1)S(1)}, u32[]{:S(2)}, u32[]{:S(2)}) %collective-permute-start.46) | collective-permute-done | bytes 262176 | tf_op jit(solution)/shard_map/ppermute | solution.py:213
  214.0 5.9 %collective-permute-done.42.refs_7_ = bf16[256,1024]{1,0:T(8,128)(2,1)} collective-permute-done((bf16[256,1024]{1,0:T(8,128)(2,1)}, bf16[256,1024]{1,0:T(8,128)(2,1)}, u32[]{:S(2)}, u32[]{:S(2)}) %collective-permute-start.42) | collective-permute-done | bytes 524320 | tf_op jit(solution)/shard_map/ppermute | solution.py:213
  219.9 4.1 %collective-permute-done.43.refs_8_ = bf16[128,1024]{1,0:T(8,128)(2,1)} collective-permute-done((bf16[128,1024]{1,0:T(8,128)(2,1)}, bf16[128,1024]{1,0:T(8,128)(2,1)}, u32[]{:S(2)}, u32[]{:S(2)}) %collective-permute-start.43) | collective-permute-done | bytes 262176 | tf_op jit(solution)/shard_map/ppermute | solution.py:213
  224.0 2.8 %collective-permute-done.44.refs_9_ = bf16[128,1024]{1,0:T(8,128)(2,1)} collective-permute-done((bf16[128,1024]{1,0:T(8,128)(2,1)}, bf16[128,1024]{1,0:T(8,128)(2,1)}, u32[]{:S(2)}, u32[]{:S(2)}) %collective-permute-start.44) | collective-permute-done | bytes 262176 | tf_op jit(solution)/shard_map/ppermute | solution.py:213
  227.8 11.2 %step_top.1 = f32[256,1024]{1,0:T(8,128)} custom-call(s32[10]{0:T(128)S(1)} %stack.62.left_at, s32[16]{0:T(128)S(1)} %stack.79.right_at, bf16[256,1024]{1,0:T(8,128)(2,1)S(1)} %copy-done.4, bf16[256,1024]{1,0:T(8,128)(2,1)} %collective-permute-done.31.refs_1_, bf16[256,1024]{1,0:T(8,128)(2,1)} %collective-permute-done.32.refs_2_, ...), custom_call_target="tpu_custom_call" | custom-call | flops 4294967296 | bytes 20971520 | tf_op jit(solution)/shard_map/step_top/pallas_call | solution.py:175
  239.1 10.4 %step_bottom.1 = f32[256,1024]{1,0:T(8,128)} custom-call(s32[10]{0:T(128)S(1)} %stack.62.left_at, s32[16]{0:T(128)S(1)} %stack.79.right_at, bf16[256,1024]{1,0:T(8,128)(2,1)S(1)} %square_bottom.1.refs_0_, bf16[256,1024]{1,0:T(8,128)(2,1)S(1)} %copy-done.10, bf16[256,1024]{1,0:T(8,128)(2,1)S(1)} %copy-done.12, ...), custom_call_target="tpu_custom_call" | custom-call | flops 4294967296 | bytes 20971520 | tf_op jit(solution)/shard_map/step_bottom/pallas_call | solution.py:175
  249.6 2.8 %pad_maximum_fusion = f32[512,1024]{1,0:T(8,128)} fusion(f32[256,1024]{1,0:T(8,128)} %step_bottom.1, f32[256,1024]{1,0:T(8,128)S(1)} %copy-done.39), kind=kLoop, calls=%fused_computation | loop fusion | flops 524288 | bytes 4194304 | tf_op jit(solution)/shard_map/concatenate | solution.py:340
  (182 shorter events, 54.6 us)
Async XLA Ops:
  32.3 26.9 %collective-permute-start = (bf16[512,1024]{1,0:T(8,128)(2,1)S(1)}, bf16[512,1024]{1,0:T(8,128)(2,1)}, u32[]{:S(2)}, u32[]{:S(2)}) collective-permute-start(bf16[512,1024]{1,0:T(8,128)(2,1)S(1)} %unpack.1.refs_0_.refs_9_.refs_10_), channel_id=1, source_target_pairs={{0,64},{8,72},{16,80},{24,88},{32,96},{40,104},{48,112},{56,120},{... | collective-permute-start | bytes 3145736 | tf_op jit(solution)/shard_map/ppermute | solution.py:204
  33.1 26.0 %collective-permute-start.1 = (bf16[512,1024]{1,0:T(8,128)(2,1)S(1)}, bf16[512,1024]{1,0:T(8,128)(2,1)S(1)}, u32[]{:S(2)}, u32[]{:S(2)}) collective-permute-start(bf16[512,1024]{1,0:T(8,128)(2,1)S(1)} %unpack.1.refs_0_.refs_9_.refs_10_), channel_id=1, source_target_pairs={{0,1},{1,2},{2,3},{3,0},{4,5},{5,6},{6,7},{7,4},{8,9},{9,10},{10,1... | collective-permute-start | bytes 3145736 | tf_op jit(solution)/shard_map/ppermute | solution.py:213
  34.5 24.6 %collective-permute-start.2 = (bf16[512,1024]{1,0:T(8,128)(2,1)S(1)}, bf16[512,1024]{1,0:T(8,128)(2,1)S(1)}, u32[]{:S(2)}, u32[]{:S(2)}) collective-permute-start(bf16[512,1024]{1,0:T(8,128)(2,1)S(1)} %unpack.1.refs_0_.refs_9_.refs_10_), channel_id=1, source_target_pairs={{0,3},{1,0},{2,1},{3,2},{4,7},{5,4},{6,5},{7,6},{8,11},{9,8},{10,9... | collective-permute-start | bytes 3145736 | tf_op jit(solution)/shard_map/ppermute | solution.py:213
  36.4 25.4 %collective-permute-start.3 = (bf16[512,1024]{1,0:T(8,128)(2,1)S(1)}, bf16[512,1024]{1,0:T(8,128)(2,1)S(1)}, u32[]{:S(2)}, u32[]{:S(2)}) collective-permute-start(bf16[512,1024]{1,0:T(8,128)(2,1)S(1)} %unpack.1.refs_0_.refs_9_.refs_10_), channel_id=1, source_target_pairs={{0,16},{8,24},{16,32},{24,40},{32,48},{40,56},{48,0},{56,8},{64,80... | collective-permute-start | bytes 3145736 | tf_op jit(solution)/shard_map/ppermute | solution.py:204
  36.9 24.9 %collective-permute-start.4 = (bf16[512,1024]{1,0:T(8,128)(2,1)S(1)}, bf16[512,1024]{1,0:T(8,128)(2,1)S(1)}, u32[]{:S(2)}, u32[]{:S(2)}) collective-permute-start(bf16[512,1024]{1,0:T(8,128)(2,1)S(1)} %unpack.1.refs_0_.refs_9_.refs_10_), channel_id=1, source_target_pairs={{0,48},{8,56},{16,0},{24,8},{32,16},{40,24},{48,32},{56,40},{64,11... | collective-permute-start | bytes 3145736 | tf_op jit(solution)/shard_map/ppermute | solution.py:204
  61.8 13.3 %collective-permute-start.6 = (bf16[256,1024]{1,0:T(8,128)(2,1)S(1)}, bf16[256,1024]{1,0:T(8,128)(2,1)S(1)}, u32[]{:S(2)}, u32[]{:S(2)}) collective-permute-start(bf16[256,1024]{1,0:T(8,128)(2,1)S(1)} %slice.57), channel_id=1, source_target_pairs={{0,1},{1,2},{2,3},{3,0},{4,5},{5,6},{6,7},{7,4},{8,9},{9,10},{10,1... | collective-permute-start | bytes 1572872 | tf_op jit(solution)/shard_map/ppermute | solution.py:213
  62.3 13.7 %collective-permute-start.7 = (bf16[256,1024]{1,0:T(8,128)(2,1)S(1)}, bf16[256,1024]{1,0:T(8,128)(2,1)S(1)}, u32[]{:S(2)}, u32[]{:S(2)}) collective-permute-start(bf16[256,1024]{1,0:T(8,128)(2,1)S(1)} %slice.58), channel_id=1, source_target_pairs={{0,3},{1,0},{2,1},{3,2},{4,7},{5,4},{6,5},{7,6},{8,11},{9,8},{10,9... | collective-permute-start | bytes 1572872 | tf_op jit(solution)/shard_map/ppermute | solution.py:213
  66.5 12.7 %collective-permute-start.13 = (bf16[256,1024]{1,0:T(8,128)(2,1)S(1)}, bf16[256,1024]{1,0:T(8,128)(2,1)S(1)}, u32[]{:S(2)}, u32[]{:S(2)}) collective-permute-start(bf16[256,1024]{1,0:T(8,128)(2,1)S(1)} %slice.59), channel_id=1, source_target_pairs={{0,16},{8,24},{16,32},{24,40},{32,48},{40,56},{48,0},{56,8},{64,80... | collective-permute-start | bytes 1572872 | tf_op jit(solution)/shard_map/ppermute | solution.py:204
  66.6 15.7 %collective-permute-start.14 = (bf16[256,1024]{1,0:T(8,128)(2,1)S(1)}, bf16[256,1024]{1,0:T(8,128)(2,1)S(1)}, u32[]{:S(2)}, u32[]{:S(2)}) collective-permute-start(bf16[256,1024]{1,0:T(8,128)(2,1)S(1)} %slice.60), channel_id=1, source_target_pairs={{0,48},{8,56},{16,0},{24,8},{32,16},{40,24},{48,32},{56,40},{64,11... | collective-permute-start | bytes 1572872 | tf_op jit(solution)/shard_map/ppermute | solution.py:204
  79.0 23.3 %collective-permute-start.11 = (bf16[512,1024]{1,0:T(8,128)(2,1)}, bf16[512,1024]{1,0:T(8,128)(2,1)}, u32[]{:S(2)}, u32[]{:S(2)}) collective-permute-start(bf16[512,1024]{1,0:T(8,128)(2,1)} %collective-permute-done.refs_19_.refs_20_), channel_id=1, source_target_pairs={{0,16},{8,24},{16,32},{24,40},{32,48},{40,56},{48,0},{56,8},{64,80... | collective-permute-start | bytes 3145736 | tf_op jit(solution)/shard_map/ppermute | solution.py:204
  79.2 23.3 %collective-permute-start.12 = (bf16[512,1024]{1,0:T(8,128)(2,1)}, bf16[512,1024]{1,0:T(8,128)(2,1)}, u32[]{:S(2)}, u32[]{:S(2)}) collective-permute-start(bf16[512,1024]{1,0:T(8,128)(2,1)} %collective-permute-done.refs_19_.refs_20_), channel_id=1, source_target_pairs={{0,48},{8,56},{16,0},{24,8},{32,16},{40,24},{48,32},{56,40},{64,11... | collective-permute-start | bytes 3145736 | tf_op jit(solution)/shard_map/ppermute | solution.py:204
  87.9 28.3 %collective-permute-start.18 = (bf16[512,1024]{1,0:T(8,128)(2,1)S(1)}, bf16[512,1024]{1,0:T(8,128)(2,1)S(1)}, u32[]{:S(2)}, u32[]{:S(2)}) collective-permute-start(bf16[512,1024]{1,0:T(8,128)(2,1)S(1)} %collective-permute-done.3.refs_11_.refs_12_), channel_id=1, source_target_pairs={{0,8},{8,0},{16,24},{24,16},{32,40},{40,32},{48,56},{56,48},{64,72... | collective-permute-start | bytes 3145736 | tf_op jit(solution)/shard_map/ppermute | solution.py:204
  90.8 27.1 %collective-permute-start.19 = (bf16[512,1024]{1,0:T(8,128)(2,1)S(1)}, bf16[512,1024]{1,0:T(8,128)(2,1)S(1)}, u32[]{:S(2)}, u32[]{:S(2)}) collective-permute-start(bf16[512,1024]{1,0:T(8,128)(2,1)S(1)} %collective-permute-done.4.refs_13_.refs_14_), channel_id=1, source_target_pairs={{0,8},{8,0},{16,24},{24,16},{32,40},{40,32},{48,56},{56,48},{64,72... | collective-permute-start | bytes 3145736 | tf_op jit(solution)/shard_map/ppermute | solution.py:204
  92.3 28.4 %collective-permute-start.17 = (bf16[512,1024]{1,0:T(8,128)(2,1)S(1)}, bf16[512,1024]{1,0:T(8,128)(2,1)S(1)}, u32[]{:S(2)}, u32[]{:S(2)}) collective-permute-start(bf16[512,1024]{1,0:T(8,128)(2,1)S(1)} %unpack.1.refs_0_.refs_9_.refs_10_), channel_id=1, source_target_pairs={{0,8},{8,0},{16,24},{24,16},{32,40},{40,32},{48,56},{56,48},{64,72... | collective-permute-start | bytes 3145736 | tf_op jit(solution)/shard_map/ppermute | solution.py:204
  131.0 19.4 %collective-permute-start.33 = (bf16[128,1024]{1,0:T(8,128)(2,1)S(1)}, bf16[128,1024]{1,0:T(8,128)(2,1)S(1)}, u32[]{:S(2)}, u32[]{:S(2)}) collective-permute-start(bf16[128,1024]{1,0:T(8,128)(2,1)S(1)} %slice.65), channel_id=1, source_target_pairs={{0,1},{1,2},{2,3},{3,0},{4,5},{5,6},{6,7},{7,4},{8,9},{9,10},{10,1... | collective-permute-start | bytes 786440 | tf_op jit(solution)/shard_map/ppermute | solution.py:213
  132.7 17.7 %collective-permute-start.34 = (bf16[128,1024]{1,0:T(8,128)(2,1)S(1)}, bf16[128,1024]{1,0:T(8,128)(2,1)S(1)}, u32[]{:S(2)}, u32[]{:S(2)}) collective-permute-start(bf16[128,1024]{1,0:T(8,128)(2,1)S(1)} %slice.66), channel_id=1, source_target_pairs={{0,3},{1,0},{2,1},{3,2},{4,7},{5,4},{6,5},{7,6},{8,11},{9,8},{10,9... | collective-permute-start | bytes 786440 | tf_op jit(solution)/shard_map/ppermute | solution.py:213
  147.1 17.1 %collective-permute-start.31 = (bf16[256,1024]{1,0:T(8,128)(2,1)S(1)}, bf16[256,1024]{1,0:T(8,128)(2,1)}, u32[]{:S(2)}, u32[]{:S(2)}) collective-permute-start(bf16[256,1024]{1,0:T(8,128)(2,1)S(1)} %square_top.1.refs_0_), channel_id=1, source_target_pairs={{0,1},{1,2},{2,3},{3,0},{4,5},{5,6},{6,7},{7,4},{8,9},{9,10},{10,1... | collective-permute-start | bytes 1572872 | tf_op jit(solution)/shard_map/ppermute | solution.py:213
  147.6 17.1 %collective-permute-start.32 = (bf16[256,1024]{1,0:T(8,128)(2,1)S(1)}, bf16[256,1024]{1,0:T(8,128)(2,1)}, u32[]{:S(2)}, u32[]{:S(2)}) collective-permute-start(bf16[256,1024]{1,0:T(8,128)(2,1)S(1)} %square_top.1.refs_0_), channel_id=1, source_target_pairs={{0,3},{1,0},{2,1},{3,2},{4,7},{5,4},{6,5},{7,6},{8,11},{9,8},{10,9... | collective-permute-start | bytes 1572872 | tf_op jit(solution)/shard_map/ppermute | solution.py:213
  159.3 16.1 %collective-permute-start.35 = (bf16[256,1024]{1,0:T(8,128)(2,1)S(1)}, bf16[256,1024]{1,0:T(8,128)(2,1)S(1)}, u32[]{:S(2)}, u32[]{:S(2)}) collective-permute-start(bf16[256,1024]{1,0:T(8,128)(2,1)S(1)} %square_bottom.1.refs_0_), channel_id=1, source_target_pairs={{0,1},{1,2},{2,3},{3,0},{4,5},{5,6},{6,7},{7,4},{8,9},{9,10},{10,1... | collective-permute-start | bytes 1572872 | tf_op jit(solution)/shard_map/ppermute | solution.py:213
  159.4 16.1 %collective-permute-start.36 = (bf16[256,1024]{1,0:T(8,128)(2,1)S(1)}, bf16[256,1024]{1,0:T(8,128)(2,1)S(1)}, u32[]{:S(2)}, u32[]{:S(2)}) collective-permute-start(bf16[256,1024]{1,0:T(8,128)(2,1)S(1)} %square_bottom.1.refs_0_), channel_id=1, source_target_pairs={{0,3},{1,0},{2,1},{3,2},{4,7},{5,4},{6,5},{7,6},{8,11},{9,8},{10,9... | collective-permute-start | bytes 1572872 | tf_op jit(solution)/shard_map/ppermute | solution.py:213
  162.6 15.0 %collective-permute-start.37 = (bf16[256,1024]{1,0:T(8,128)(2,1)S(1)}, bf16[256,1024]{1,0:T(8,128)(2,1)}, u32[]{:S(2)}, u32[]{:S(2)}) collective-permute-start(bf16[256,1024]{1,0:T(8,128)(2,1)S(1)} %square_bottom.1.refs_0_), channel_id=1, source_target_pairs={{0,4},{1,5},{2,6},{3,7},{4,0},{5,1},{6,2},{7,3},{8,12},{9,13},{10,... | collective-permute-start | bytes 1572872 | tf_op jit(solution)/shard_map/ppermute | solution.py:213
  164.2 22.3 %collective-permute-start.40 = (bf16[256,1024]{1,0:T(8,128)(2,1)S(1)}, bf16[256,1024]{1,0:T(8,128)(2,1)S(1)}, u32[]{:S(2)}, u32[]{:S(2)}) collective-permute-start(bf16[256,1024]{1,0:T(8,128)(2,1)S(1)} %square_top.1.refs_0_), channel_id=1, source_target_pairs={{0,4},{1,5},{2,6},{3,7},{4,0},{5,1},{6,2},{7,3},{8,12},{9,13},{10,... | collective-permute-start | bytes 1572872 | tf_op jit(solution)/shard_map/ppermute | solution.py:213
  165.7 21.6 %collective-permute-start.38 = (bf16[128,1024]{1,0:T(8,128)(2,1)S(1)}, bf16[128,1024]{1,0:T(8,128)(2,1)}, u32[]{:S(2)}, u32[]{:S(2)}) collective-permute-start(bf16[128,1024]{1,0:T(8,128)(2,1)S(1)} %slice.67), channel_id=1, source_target_pairs={{0,1},{1,2},{2,3},{3,0},{4,5},{5,6},{6,7},{7,4},{8,9},{9,10},{10,1... | collective-permute-start | bytes 786440 | tf_op jit(solution)/shard_map/ppermute | solution.py:213
  188.1 20.2 %collective-permute-start.47 = (bf16[256,1024]{1,0:T(8,128)(2,1)}, bf16[256,1024]{1,0:T(8,128)(2,1)S(1)}, u32[]{:S(2)}, u32[]{:S(2)}) collective-permute-start(bf16[256,1024]{1,0:T(8,128)(2,1)} %collective-permute-done.37.refs_5_), channel_id=1, source_target_pairs={{0,1},{1,2},{2,3},{3,0},{4,5},{5,6},{6,7},{7,4},{8,9},{9,10},{10,1... | collective-permute-start | bytes 1572872 | tf_op jit(solution)/shard_map/ppermute | solution.py:213
  188.1 20.8 %collective-permute-start.48 = (bf16[256,1024]{1,0:T(8,128)(2,1)}, bf16[256,1024]{1,0:T(8,128)(2,1)}, u32[]{:S(2)}, u32[]{:S(2)}) collective-permute-start(bf16[256,1024]{1,0:T(8,128)(2,1)} %collective-permute-done.37.refs_5_), channel_id=1, source_target_pairs={{0,3},{1,0},{2,1},{3,2},{4,7},{5,4},{6,5},{7,6},{8,11},{9,8},{10,9... | collective-permute-start | bytes 1572872 | tf_op jit(solution)/shard_map/ppermute | solution.py:213
  191.4 14.7 %collective-permute-start.46 = (bf16[128,1024]{1,0:T(8,128)(2,1)S(1)}, bf16[128,1024]{1,0:T(8,128)(2,1)S(1)}, u32[]{:S(2)}, u32[]{:S(2)}) collective-permute-start(bf16[128,1024]{1,0:T(8,128)(2,1)S(1)} %slice.70), channel_id=1, source_target_pairs={{0,3},{1,0},{2,1},{3,2},{4,7},{5,4},{6,5},{7,6},{8,11},{9,8},{10,9... | collective-permute-start | bytes 786440 | tf_op jit(solution)/shard_map/ppermute | solution.py:213
  193.5 18.5 %collective-permute-start.41 = (bf16[256,1024]{1,0:T(8,128)(2,1)}, bf16[256,1024]{1,0:T(8,128)(2,1)}, u32[]{:S(2)}, u32[]{:S(2)}) collective-permute-start(bf16[256,1024]{1,0:T(8,128)(2,1)} %collective-permute-done.31.refs_1_), channel_id=1, source_target_pairs={{0,4},{1,5},{2,6},{3,7},{4,0},{5,1},{6,2},{7,3},{8,12},{9,13},{10,... | collective-permute-start | bytes 1572872 | tf_op jit(solution)/shard_map/ppermute | solution.py:213
  198.6 21.3 %collective-permute-start.42 = (bf16[256,1024]{1,0:T(8,128)(2,1)}, bf16[256,1024]{1,0:T(8,128)(2,1)}, u32[]{:S(2)}, u32[]{:S(2)}) collective-permute-start(bf16[256,1024]{1,0:T(8,128)(2,1)} %collective-permute-done.32.refs_2_), channel_id=1, source_target_pairs={{0,4},{1,5},{2,6},{3,7},{4,0},{5,1},{6,2},{7,3},{8,12},{9,13},{10,... | collective-permute-start | bytes 1572872 | tf_op jit(solution)/shard_map/ppermute | solution.py:213
  206.8 17.2 %collective-permute-start.43 = (bf16[128,1024]{1,0:T(8,128)(2,1)}, bf16[128,1024]{1,0:T(8,128)(2,1)}, u32[]{:S(2)}, u32[]{:S(2)}) collective-permute-start(bf16[128,1024]{1,0:T(8,128)(2,1)} %collective-permute-done.38.refs_3_), channel_id=1, source_target_pairs={{0,4},{1,5},{2,6},{3,7},{4,0},{5,1},{6,2},{7,3},{8,12},{9,13},{10,... | collective-permute-start | bytes 786440 | tf_op jit(solution)/shard_map/ppermute | solution.py:213
  208.3 18.4 %collective-permute-start.44 = (bf16[128,1024]{1,0:T(8,128)(2,1)}, bf16[128,1024]{1,0:T(8,128)(2,1)}, u32[]{:S(2)}, u32[]{:S(2)}) collective-permute-start(bf16[128,1024]{1,0:T(8,128)(2,1)} %collective-permute-done.39.refs_4_), channel_id=1, source_target_pairs={{0,4},{1,5},{2,6},{3,7},{4,0},{5,1},{6,2},{7,3},{8,12},{9,13},{10,... | collective-permute-start | bytes 786440 | tf_op jit(solution)/shard_map/ppermute | solution.py:213
  208.9 30.1 %collective-permute-start.49 = (bf16[128,1024]{1,0:T(8,128)(2,1)S(1)}, bf16[128,1024]{1,0:T(8,128)(2,1)S(1)}, u32[]{:S(2)}, u32[]{:S(2)}) collective-permute-start(bf16[128,1024]{1,0:T(8,128)(2,1)S(1)} %slice.71), channel_id=1, source_target_pairs={{0,1},{1,2},{2,3},{3,0},{4,5},{5,6},{6,7},{7,4},{8,9},{9,10},{10,1... | collective-permute-start | bytes 786440 | tf_op jit(solution)/shard_map/ppermute | solution.py:213
  212.0 27.1 %collective-permute-start.50 = (bf16[128,1024]{1,0:T(8,128)(2,1)S(1)}, bf16[128,1024]{1,0:T(8,128)(2,1)S(1)}, u32[]{:S(2)}, u32[]{:S(2)}) collective-permute-start(bf16[128,1024]{1,0:T(8,128)(2,1)S(1)} %slice.72), channel_id=1, source_target_pairs={{0,3},{1,0},{2,1},{3,2},{4,7},{5,4},{6,5},{7,6},{8,11},{9,8},{10,9... | collective-permute-start | bytes 786440 | tf_op jit(solution)/shard_map/ppermute | solution.py:213
  (61 other events, 914.3 us)
